TPU v7x, 32 devices: a whole 2x2x4 slice. The times are simulated.
32 devices in a mesh: row: 8 (over y, x, core), col: 4 (over z).
Axes of the slice: x: 2, y: 2, z: 4, core: 2. Of those that a mesh axis runs over, the one named last changes fastest.
Arguments:
- slip_rate: bfloat16 [32, 8, 128, 256], P('row', 'col'), may hold values from -6 to 6
- near_lists: int32 [32, 8, 6], P('row', 'col'), may hold values from 0 to 8, as said below
- near_blocks: bfloat16 [32, 8, 6, 128, 128], P('row', 'col'), may hold values from -0.21875 to 0.21875
- source_basis: bfloat16 [32, 8, 64, 128], P('row', 'col'), may hold values from -0.5 to 0.5
- target_basis: bfloat16 [32, 8, 64, 128], P('row', 'col'), may hold values from -0.75 to 0.75
- leaf_up: float32 [32, 8, 64, 64], P('row', 'col'), may hold values from -0.25 to 0.25
- leaf_down: float32 [32, 8, 64, 64], P('row', 'col'), may hold values from -0.75 to 0.75
- strip_up: float32 [8, 2, 2, 64, 64], P('row'), may hold values from -0.5 to 0.5
- strip_down: float32 [8, 2, 2, 64, 64], P('row'), may hold values from -0.75 to 0.75
- strip_lists: int32 [8, 4], P('row'), may hold values from 0 to 7, as said below
- coupling: float32 [8, 4, 64, 64], P('row'), may hold values from -0.375 to 0.375
Outputs:
- stress_rate: bfloat16 [32, 8, 128, 256], P('row', 'col')
Inputs may be any that keep to these rules, and one draw needn't show every extreme that they name: `near_lists`: entry q names the neighbour leaf at offset (q // 3 - 1, q % 3 - 1); the first entry of every leaf is 4, its own block; the 6 entries of one leaf are distinct. `strip_lists`: strip r lists 4 distinct strips s with |s - r| >= 2.
All inputs are finite; a program needn't handle non-finite values.
Results may differ from a plain program's by a relative error of at most 0.0047.
Values may be sent and summed in bfloat16 or wider, within the bound.
A program may use at most 64 MiB of HBM per device.

v0:
```python
import functools

import jax
import jax.numpy as jnp
from jax import lax
from jax.experimental import pallas as pl
from jax.experimental.pallas import tpu as pltpu
from jax.sharding import PartitionSpec as P

F32, BF16 = jnp.float32, jnp.bfloat16
MESH = pl.DeviceIdType.MESH


def dot(a, b):
    return jnp.dot(a, b, preferred_element_type=F32)


def split(x):
    high = x.astype(BF16)
    return high, (x - high.astype(F32)).astype(BF16)


def dot3(a, b):
    a_high, a_low = split(a)
    b_high, b_low = split(b)
    return dot(a_high, b_high) + (dot(a_high, b_low) + dot(a_low, b_high))


def kernel(
    n_row,
    n_col,
    lists_hbm,
    strips_hbm,
    slip_hbm,
    near_hbm,
    source_hbm,
    target_hbm,
    up_hbm,
    down_hbm,
    strip_up_hbm,
    strip_down_hbm,
    coupling_hbm,
    out_hbm,
    lists,
    strips,
    out,
    pad,
    near,
    source,
    target,
    up,
    down,
    strip_up,
    strip_down,
    coupling,
    acc,
    part_send,
    part_recv,
    tops,
    coeff,
    fall,
    spread,
    pair_high,
    pair_low,
    load_sem,
    halo_send,
    halo_recv,
    part_sems,
    part_rsems,
    top_sems,
    top_rsems,
    coeff_sems,
    out_sems,
):
    along, dip = slip_hbm.shape[:2]
    rank = source.shape[2]
    levels = strip_up.shape[1]
    n_far = coupling.shape[1]
    n_near = lists.shape[2]
    half = part_send.shape[2]
    row, col = lax.axis_index("row"), lax.axis_index("col")

    barrier = pltpu.get_barrier_semaphore()
    for j in range(1, n_row):
        pl.semaphore_signal(barrier, inc=1, device_id={"row": lax.rem(row + j, n_row)}, device_id_type=MESH)
    for j in range(1, n_col):
        pl.semaphore_signal(barrier, inc=1, device_id={"col": lax.rem(col + j, n_col)}, device_id_type=MESH)

    loads = [
        pltpu.make_async_copy(src, dst, load_sem.at[k])
        for k, (src, dst) in enumerate(
            [
                (strip_up_hbm, strip_up),
                (up_hbm, up),
                (source_hbm, source),
                (slip_hbm, pad.at[pl.ds(1, along), pl.ds(1, dip)]),
                (lists_hbm, lists),
                (strips_hbm, strips),
                (near_hbm, near.at[:, :, pl.ds(0, n_near)]),
                (coupling_hbm, coupling),
                (strip_down_hbm, strip_down),
                (down_hbm, down),
                (target_hbm, target),
            ]
        )
    ]
    for load in loads:
        load.start()

    has = {"W": col > 0, "E": col < n_col - 1, "N": row > 0, "S": row < n_row - 1}
    there = {"W": {"col": col - 1}, "E": {"col": col + 1}, "N": {"row": row - 1}, "S": {"row": row + 1}}
    back = {"W": "E", "E": "W", "N": "S", "S": "N"}
    slot_of = {}

    def halo(name, side, src, dst):
        k = slot_of.setdefault(name, len(slot_of))
        return pltpu.make_async_remote_copy(
            src_ref=src, dst_ref=dst, send_sem=halo_send.at[k], recv_sem=halo_recv.at[k],
            device_id=there[side], device_id_type=MESH,
        )

    def rim(side, g, n):
        src = slip_hbm.at[pl.ds(g, n), pl.ds(0 if side == "W" else dip - 1, 1)]
        dst = pad.at[pl.ds(1 + g, n), pl.ds(dip + 1 if side == "W" else 0, 1)]
        return halo((side, g), side, src, dst)

    def strike(side):
        src = slip_hbm.at[pl.ds(0 if side == "N" else along - 1, 1)]
        dst = pad.at[pl.ds(along + 1 if side == "N" else 0, 1), pl.ds(1, dip)]
        return halo((side, "own"), side, src, dst)

    def corner(side, edge):
        at = 0 if edge == "W" else dip + 1
        src = pad.at[pl.ds(1 if side == "N" else along, 1), pl.ds(at, 1)]
        dst = pad.at[pl.ds(along + 1 if side == "N" else 0, 1), pl.ds(at, 1)]
        return halo((side, edge), side, src, dst)

    first_rim = [(0, 1), (along - 1, 1)]
    later_rim = [(1, along - 2)]

    pl.semaphore_wait(barrier, n_row + n_col - 2)

    for g, n in first_rim:
        for side in "WE":
            pl.when(has[side])(lambda: rim(side, g, n).start())
    for side in "NS":
        pl.when(has[side])(lambda: strike(side).start())

    empty = jnp.zeros((along + 2, 1) + pad.shape[2:], pad.dtype)
    for side, at in (("W", 0), ("E", dip + 1)):
        @pl.when(jnp.logical_not(has[side]))
        def _():
            pad[:, pl.ds(at, 1)] = empty
    for side, at in (("N", 0), ("S", along + 1)):
        @pl.when(jnp.logical_not(has[side]))
        def _():
            pad[pl.ds(at, 1)] = jnp.zeros((1,) + pad.shape[1:], pad.dtype)
    near[:, :, n_near] = jnp.zeros((along, dip) + near.shape[3:], near.dtype)

    leaves = [(g, h) for g in range(along) for h in range(dip)]
    loads[0].wait()
    lift = strip_up[0, 0, lax.rem(col, 2)]
    for level in range(1, levels):
        lift = dot3(strip_up[0, level, lax.rem(col // 2**level, 2)], lift)
    loads[1].wait()
    gather_up = jnp.concatenate([up[g, h] for g, h in leaves], axis=1)
    loads[2].wait()
    loads[3].wait()
    moments = jnp.concatenate([dot(source[g, h], pad[g + 1, h + 1]) for g, h in leaves], axis=0)
    lifted = dot3(lift, dot3(gather_up, moments))
    for k in range(2):
        part_send[k] = lifted[:, k * half : (k + 1) * half].astype(part_send.dtype)

    def part(j):
        to = lax.rem(col + j, n_col)
        return pltpu.make_async_remote_copy(
            src_ref=part_send.at[lax.rem(to, 2)], dst_ref=part_recv.at[j],
            send_sem=part_sems.at[j], recv_sem=part_rsems.at[j],
            device_id={"col": to}, device_id_type=MESH,
        )

    for j in range(1, n_col):
        part(j).start()
    for g, n in later_rim:
        for side in "WE":
            pl.when(has[side])(lambda: rim(side, g, n).start())

    for load in loads[7:]:
        load.wait()
    pair_high[...], pair_low[...] = split(jnp.concatenate([coupling[0, a] for a in range(n_far)], axis=1))
    lower = strip_down[0, levels - 1, lax.rem(col // 2 ** (levels - 1), 2)]
    for level in reversed(range(levels - 1)):
        lower = dot3(strip_down[0, level, lax.rem(col // 2**level, 2)], lower)
    fall_high, fall_low = split(dot3(down[...].reshape(along * dip * rank, rank), lower))
    fall[...] = jnp.concatenate([fall_high, fall_low, fall_high], axis=1)
    for g, h in leaves:
        spread[g, h] = target[g, h].astype(F32).T.astype(BF16)

    for load in loads[4:7]:
        load.wait()

    def place(g, h, q):
        index = n_near
        for n in range(n_near):
            index = jnp.where(lists[g, h, n] == q, n, index)
        return index

    def wave(g, h, wanted):
        found = [
            (q, g + q // 3, h + q % 3)
            for q in range(9)
            if wanted == (1 <= g + q // 3 <= along, 1 <= h + q % 3 <= dip)
        ]
        if not found:
            return None
        blocks = jnp.concatenate([near[g, h, place(g, h, q)] for q, _, _ in found], axis=1)
        fields = jnp.concatenate([pad[a, b] for _, a, b in found], axis=0)
        return dot(blocks, fields)

    for g, h in leaves[: len(leaves) // 2]:
        acc[g, h] = wave(g, h, (True, True))

    for g, n in first_rim:
        for side in "WE":
            pl.when(has[back[side]])(lambda: rim(side, g, n).wait_recv())
    for edge in "WE":
        for side in "NS":
            pl.when(jnp.logical_and(has[side], has[edge]))(lambda: corner(side, edge).start())

    for j in range(1, n_col):
        part(j).wait_recv()
    mine = lax.rem(col, 2)
    total = part_send[mine].astype(F32)
    for j in range(1, n_col):
        total = total + part_recv[j].astype(F32)
    tops[row] = total.astype(tops.dtype)

    def top(j, owner):
        return pltpu.make_async_remote_copy(
            src_ref=tops.at[owner], dst_ref=tops.at[owner],
            send_sem=top_sems.at[j], recv_sem=top_rsems.at[j],
            device_id={"row": lax.rem(row + j, n_row)}, device_id_type=MESH,
        )

    for j in range(1, n_row):
        top(j, row).start()

    for g, h in leaves[len(leaves) // 2 :]:
        acc[g, h] = wave(g, h, (True, True))

    for j in range(1, n_row):
        top(j, lax.rem(row + n_row - j, n_row)).wait_recv()
    chosen = jnp.concatenate([tops[strips[0, a]] for a in range(n_far)], axis=0)
    coeff[mine] = dot(pair_high[...], chosen) + dot(pair_low[...], chosen)

    def swap(side):
        return pltpu.make_async_remote_copy(
            src_ref=coeff.at[side], dst_ref=coeff.at[side],
            send_sem=coeff_sems.at[0], recv_sem=coeff_sems.at[1],
            device_id={"col": col + 1 - 2 * mine}, device_id_type=MESH,
        )

    swap(mine).start()

    for g, n in later_rim:
        for side in "WE":
            pl.when(has[back[side]])(lambda: rim(side, g, n).wait_recv())
    for g, h in leaves:
        acc[g, h] += wave(g, h, (True, False))
    for side in "NS":
        pl.when(has[back[side]])(lambda: strike(side).wait_recv())
    for g, h in leaves:
        if g in (0, along - 1):
            acc[g, h] += wave(g, h, (False, True))

    swap(1 - mine).wait_recv()
    c_high, c_low = split(jnp.concatenate([coeff[0], coeff[1]], axis=1))
    falls = dot(fall[...], jnp.concatenate([c_high, c_high, c_low], axis=0)).astype(BF16)

    def result(g, h):
        return pltpu.make_async_copy(out.at[g, h], out_hbm.at[g, h], out_sems.at[g, h])

    def finish(g, h, value):
        k = g * dip + h
        out[g, h] = (value + dot(spread[g, h], falls[k * rank : (k + 1) * rank])).astype(out.dtype)
        result(g, h).start()

    for g, h in leaves:
        if g not in (0, along - 1):
            finish(g, h, acc[g, h])
    for edge in "WE":
        for side in "NS":
            pl.when(jnp.logical_and(has[back[side]], has[edge]))(lambda: corner(side, edge).wait_recv())
    for g, h in leaves:
        if g in (0, along - 1):
            finish(g, h, acc[g, h] + wave(g, h, (False, False)))

    for g, n in first_rim + later_rim:
        for side in "WE":
            pl.when(has[side])(lambda: rim(side, g, n).wait_send())
    for side in "NS":
        pl.when(has[side])(lambda: strike(side).wait_send())
        for edge in "WE":
            pl.when(jnp.logical_and(has[side], has[edge]))(lambda: corner(side, edge).wait_send())
    for j in range(1, n_col):
        part(j).wait_send()
    for j in range(1, n_row):
        top(j, row).wait_send()
    swap(mine).wait_send()
    for g, h in leaves:
        result(g, h).wait()


def body(
    n_row,
    n_col,
    slip_rate,
    near_lists,
    near_blocks,
    source_basis,
    target_basis,
    leaf_up,
    leaf_down,
    strip_up,
    strip_down,
    strip_lists,
    coupling,
):
    along, dip, leaf, members = slip_rate.shape
    rank = source_basis.shape[2]
    n_near = near_lists.shape[2]
    n_far = coupling.shape[1]
    half = members // 2
    whole = pl.BlockSpec(memory_space=pltpu.HBM)
    dma = pltpu.SemaphoreType.DMA
    operands = [
        near_lists,
        strip_lists,
        slip_rate,
        near_blocks,
        source_basis,
        target_basis,
        leaf_up,
        leaf_down,
        strip_up,
        strip_down,
        coupling,
    ]
    pinned = [pltpu.with_memory_space_constraint(x, pltpu.HBM) for x in operands]
    return pl.pallas_call(
        functools.partial(kernel, n_row, n_col),
        out_shape=jax.ShapeDtypeStruct(slip_rate.shape, BF16),
        in_specs=[whole] * 11,
        out_specs=pl.BlockSpec(memory_space=pl.ANY),
        scratch_shapes=[
            pltpu.SMEM(near_lists.shape, jnp.int32),
            pltpu.SMEM(strip_lists.shape, jnp.int32),
            pltpu.VMEM(slip_rate.shape, BF16),
            pltpu.VMEM((along + 2, dip + 2, leaf, members), BF16),
            pltpu.VMEM((along, dip, n_near + 1, leaf, leaf), BF16),
            pltpu.VMEM(source_basis.shape, BF16),
            pltpu.VMEM(target_basis.shape, BF16),
            pltpu.VMEM(leaf_up.shape, F32),
            pltpu.VMEM(leaf_down.shape, F32),
            pltpu.VMEM(strip_up.shape, F32),
            pltpu.VMEM(strip_down.shape, F32),
            pltpu.VMEM(coupling.shape, F32),
            pltpu.VMEM(slip_rate.shape, F32),
            pltpu.VMEM((2, rank, half), BF16),
            pltpu.VMEM((n_col, rank, half), BF16),
            pltpu.VMEM((n_row, rank, half), BF16),
            pltpu.VMEM((2, rank, half), F32),
            pltpu.VMEM((along * dip * rank, 3 * rank), BF16),
            pltpu.VMEM((along, dip, leaf, rank), BF16),
            pltpu.VMEM((rank, n_far * rank), BF16),
            pltpu.VMEM((rank, n_far * rank), BF16),
            dma((11,)),
            dma((12,)),
            dma((12,)),
            dma((n_col,)),
            dma((n_col,)),
            dma((n_row,)),
            dma((n_row,)),
            dma((2,)),
            dma((along, dip)),
        ],
        compiler_params=pltpu.CompilerParams(
            collective_id=0, has_side_effects=True, vmem_limit_bytes=40 * 1024 * 1024
        ),
    )(*pinned)


def solution(mesh):
    in_specs = (
        P("row", "col", None, None),
        P("row", "col", None),
        P("row", "col", None, None, None),
        P("row", "col", None, None),
        P("row", "col", None, None),
        P("row", "col", None, None),
        P("row", "col", None, None),
        P("row", None, None, None, None),
        P("row", None, None, None, None),
        P("row", None),
        P("row", None, None, None),
    )
    out_specs = P("row", "col", None, None)
    run = functools.partial(body, mesh.shape["row"], mesh.shape["col"])
    return jax.shard_map(run, mesh=mesh, in_specs=in_specs, out_specs=out_specs, check_vma=False)
```

profile of v0, /device:TPU:0, one launch (start us, length us, event | category | flops | bytes accessed | tf_op | source)
XLA Modules:
  0.0 23.1 jit_solution(6003724335872111489)
XLA Ops:
  0.0 22.3 %shard_map.109 = bf16[4,2,128,256]{3,2,1,0:T(8,128)(2,1)S(1)} custom-call(s32[4,2,6]{2,1,0:T(2,128)} %lists_hbm.1, s32[1,4]{1,0:T(1,128)} %strips_hbm.1, bf16[4,2,128,256]{3,2,1,0:T(8,128)(2,1)} %slip_hbm.1, bf16[4,2,6,128,128]{4,3,2,1,0:T(8,128)(2,1)} %near_hbm.1, bf16[4,2,64,128]{3,2,1,0:T(8,128)(2,1)} %source_hbm.1, bf16[4,2,64,128]{3,2,1,0:T(8,128)(2,1)} %target_hbm.1, ...), custom_call_target="tpu_custom_call" | custom-call | tf_op jit(solution)/shard_map/pallas_call | solution.py:350
  22.3 0.8 %copy.13 = bf16[4,2,128,256]{3,2,1,0:T(8,128)(2,1)} copy(bf16[4,2,128,256]{3,2,1,0:T(8,128)(2,1)S(1)} %shard_map.109) | data formatting | bytes 1048576
where the time goes:
time: 23.2 us; the launch traced here: 23.1 us
  Pallas kernels  22.3 us (96%)
  local copies, waits for them, and re-layouts  0.8 us (3%)
    pallas_call x1, Pallas kernels, body(): pl.pallas_call(functools.partial(kernel, n_row, n_col), out_shape=jax.Sha...  22.3 us
    unnamed x1, local copies, waits for them, and re-layouts  0.8 us

commit v1 on v0

--- a/solution.py
+++ b/solution.py
@@ -143,8 +143,6 @@
     for g, n in first_rim:
         for side in "WE":
             pl.when(has[side])(lambda: rim(side, g, n).start())
-    for side in "NS":
-        pl.when(has[side])(lambda: strike(side).start())
 
     empty = jnp.zeros((along + 2, 1) + pad.shape[2:], pad.dtype)
     for side, at in (("W", 0), ("E", dip + 1)):
@@ -181,9 +179,8 @@
 
     for j in range(1, n_col):
         part(j).start()
-    for g, n in later_rim:
-        for side in "WE":
-            pl.when(has[side])(lambda: rim(side, g, n).start())
+    for side in "NS":
+        pl.when(has[side])(lambda: strike(side).start())
 
     for load in loads[7:]:
         load.wait()
@@ -220,13 +217,6 @@
     for g, h in leaves[: len(leaves) // 2]:
         acc[g, h] = wave(g, h, (True, True))
 
-    for g, n in first_rim:
-        for side in "WE":
-            pl.when(has[back[side]])(lambda: rim(side, g, n).wait_recv())
-    for edge in "WE":
-        for side in "NS":
-            pl.when(jnp.logical_and(has[side], has[edge]))(lambda: corner(side, edge).start())
-
     for j in range(1, n_col):
         part(j).wait_recv()
     mine = lax.rem(col, 2)
@@ -244,6 +234,16 @@
 
     for j in range(1, n_row):
         top(j, row).start()
+    for g, n in later_rim:
+        for side in "WE":
+            pl.when(has[side])(lambda: rim(side, g, n).start())
+    for g, n in first_rim:
+        for side in "WE":
+            pl.when(has[back[side]])(lambda: rim(side, g, n).wait_recv())
+    for edge in "WE":
+        for side in "NS":
+            pl.when(jnp.logical_and(has[side], has[edge]))(lambda: corner(side, edge).start())
+
 
     for g, h in leaves[len(leaves) // 2 :]:
         acc[g, h] = wave(g, h, (True, True))

time: 23.2 us -> 22.2 us (0.957)
  Pallas kernels: 22.3 us -> 21.2 us
    pallas_call x1, Pallas kernels: 22.3 us -> 21.2 us  [body(): pl.pallas_call(functools.partial(kernel, n_row, n_col), out_shape=jax.Sha...]
where the time goes in v1:
time: 22.2 us; the launch traced here: 22 us
  Pallas kernels  21.2 us (95%)
  local copies, waits for them, and re-layouts  0.8 us (4%)
    pallas_call x1, Pallas kernels, body(): pl.pallas_call(functools.partial(kernel, n_row, n_col), out_shape=jax.Sha...  21.2 us
    unnamed x1, local copies, waits for them, and re-layouts  0.8 us

profile of v1, /device:TPU:0, one launch (start us, length us, event | category | flops | bytes accessed | tf_op | source)
XLA Modules:
  0.0 22.0 jit_solution(12606668580847395341)
XLA Ops:
  0.0 21.2 %shard_map.109 = bf16[4,2,128,256]{3,2,1,0:T(8,128)(2,1)S(1)} custom-call(s32[4,2,6]{2,1,0:T(2,128)} %lists_hbm.1, s32[1,4]{1,0:T(1,128)} %strips_hbm.1, bf16[4,2,128,256]{3,2,1,0:T(8,128)(2,1)} %slip_hbm.1, bf16[4,2,6,128,128]{4,3,2,1,0:T(8,128)(2,1)} %near_hbm.1, bf16[4,2,64,128]{3,2,1,0:T(8,128)(2,1)} %source_hbm.1, bf16[4,2,64,128]{3,2,1,0:T(8,128)(2,1)} %target_hbm.1, ...), custom_call_target="tpu_custom_call" | custom-call | tf_op jit(solution)/shard_map/pallas_call | solution.py:350
  21.3 0.8 %copy.13 = bf16[4,2,128,256]{3,2,1,0:T(8,128)(2,1)} copy(bf16[4,2,128,256]{3,2,1,0:T(8,128)(2,1)S(1)} %shard_map.109) | data formatting | bytes 1048576

commit v2 on v1

--- a/solution.py
+++ b/solution.py
@@ -57,7 +57,6 @@
     part_send,
     part_recv,
     tops,
-    coeff,
     fall,
     spread,
     pair_high,
@@ -69,7 +68,6 @@
     part_rsems,
     top_sems,
     top_rsems,
-    coeff_sems,
     out_sems,
 ):
     along, dip = slip_hbm.shape[:2]
@@ -77,7 +75,6 @@
     levels = strip_up.shape[1]
     n_far = coupling.shape[1]
     n_near = lists.shape[2]
-    half = part_send.shape[2]
     row, col = lax.axis_index("row"), lax.axis_index("col")
 
     barrier = pltpu.get_barrier_semaphore()
@@ -166,13 +163,12 @@
     loads[3].wait()
     moments = jnp.concatenate([dot(source[g, h], pad[g + 1, h + 1]) for g, h in leaves], axis=0)
     lifted = dot3(lift, dot3(gather_up, moments))
-    for k in range(2):
-        part_send[k] = lifted[:, k * half : (k + 1) * half].astype(part_send.dtype)
+    part_send[...] = lifted.astype(part_send.dtype)
 
     def part(j):
         to = lax.rem(col + j, n_col)
         return pltpu.make_async_remote_copy(
-            src_ref=part_send.at[lax.rem(to, 2)], dst_ref=part_recv.at[j],
+            src_ref=part_send, dst_ref=part_recv.at[j],
             send_sem=part_sems.at[j], recv_sem=part_rsems.at[j],
             device_id={"col": to}, device_id_type=MESH,
         )
@@ -219,8 +215,7 @@
 
     for j in range(1, n_col):
         part(j).wait_recv()
-    mine = lax.rem(col, 2)
-    total = part_send[mine].astype(F32)
+    total = part_send[...].astype(F32)
     for j in range(1, n_col):
         total = total + part_recv[j].astype(F32)
     tops[row] = total.astype(tops.dtype)
@@ -251,16 +246,8 @@
     for j in range(1, n_row):
         top(j, lax.rem(row + n_row - j, n_row)).wait_recv()
     chosen = jnp.concatenate([tops[strips[0, a]] for a in range(n_far)], axis=0)
-    coeff[mine] = dot(pair_high[...], chosen) + dot(pair_low[...], chosen)
-
-    def swap(side):
-        return pltpu.make_async_remote_copy(
-            src_ref=coeff.at[side], dst_ref=coeff.at[side],
-            send_sem=coeff_sems.at[0], recv_sem=coeff_sems.at[1],
-            device_id={"col": col + 1 - 2 * mine}, device_id_type=MESH,
-        )
-
-    swap(mine).start()
+    c_high, c_low = split(dot(pair_high[...], chosen) + dot(pair_low[...], chosen))
+    falls = dot(fall[...], jnp.concatenate([c_high, c_high, c_low], axis=0)).astype(BF16)
 
     for g, n in later_rim:
         for side in "WE":
@@ -272,10 +259,6 @@
     for g, h in leaves:
         if g in (0, along - 1):
             acc[g, h] += wave(g, h, (False, True))
-
-    swap(1 - mine).wait_recv()
-    c_high, c_low = split(jnp.concatenate([coeff[0], coeff[1]], axis=1))
-    falls = dot(fall[...], jnp.concatenate([c_high, c_high, c_low], axis=0)).astype(BF16)
 
     def result(g, h):
         return pltpu.make_async_copy(out.at[g, h], out_hbm.at[g, h], out_sems.at[g, h])
@@ -288,13 +271,6 @@
     for g, h in leaves:
         if g not in (0, along - 1):
             finish(g, h, acc[g, h])
-    for edge in "WE":
-        for side in "NS":
-            pl.when(jnp.logical_and(has[back[side]], has[edge]))(lambda: corner(side, edge).wait_recv())
-    for g, h in leaves:
-        if g in (0, along - 1):
-            finish(g, h, acc[g, h] + wave(g, h, (False, False)))
-
     for g, n in first_rim + later_rim:
         for side in "WE":
             pl.when(has[side])(lambda: rim(side, g, n).wait_send())
@@ -306,7 +282,13 @@
         part(j).wait_send()
     for j in range(1, n_row):
         top(j, row).wait_send()
-    swap(mine).wait_send()
+    for edge in "WE":
+        for side in "NS":
+            pl.when(jnp.logical_and(has[back[side]], has[edge]))(lambda: corner(side, edge).wait_recv())
+    for g, h in leaves:
+        if g in (0, along - 1):
+            finish(g, h, acc[g, h] + wave(g, h, (False, False)))
+
     for g, h in leaves:
         result(g, h).wait()
 
@@ -330,7 +312,6 @@
     rank = source_basis.shape[2]
     n_near = near_lists.shape[2]
     n_far = coupling.shape[1]
-    half = members // 2
     whole = pl.BlockSpec(memory_space=pltpu.HBM)
     dma = pltpu.SemaphoreType.DMA
     operands = [
@@ -366,10 +347,9 @@
             pltpu.VMEM(strip_down.shape, F32),
             pltpu.VMEM(coupling.shape, F32),
             pltpu.VMEM(slip_rate.shape, F32),
-            pltpu.VMEM((2, rank, half), BF16),
-            pltpu.VMEM((n_col, rank, half), BF16),
-            pltpu.VMEM((n_row, rank, half), BF16),
-            pltpu.VMEM((2, rank, half), F32),
+            pltpu.VMEM((rank, members), BF16),
+            pltpu.VMEM((n_col, rank, members), BF16),
+            pltpu.VMEM((n_row, rank, members), BF16),
             pltpu.VMEM((along * dip * rank, 3 * rank), BF16),
             pltpu.VMEM((along, dip, leaf, rank), BF16),
             pltpu.VMEM((rank, n_far * rank), BF16),
@@ -381,7 +361,6 @@
             dma((n_col,)),
             dma((n_row,)),
             dma((n_row,)),
-            dma((2,)),
             dma((along, dip)),
         ],
         compiler_params=pltpu.CompilerParams(

time: 22.2 us -> 21.2 us (0.955)
  Pallas kernels: 21.2 us -> 20.3 us
    pallas_call x1, Pallas kernels: 21.2 us -> 20.3 us  [body(): pl.pallas_call(functools.partial(kernel, n_row, n_col), out_shape=jax.Sha...]
where the time goes in v2:
time: 21.2 us; the launch traced here: 21.1 us
  Pallas kernels  20.3 us (96%)
  local copies, waits for them, and re-layouts  0.8 us (4%)
    pallas_call x1, Pallas kernels, body(): pl.pallas_call(functools.partial(kernel, n_row, n_col), out_shape=jax.Sha...  20.3 us
    unnamed x1, local copies, waits for them, and re-layouts  0.8 us

profile of v2, /device:TPU:0, one launch (start us, length us, event | category | flops | bytes accessed | tf_op | source)
XLA Modules:
  0.0 21.1 jit_solution(7828512527951548655)
XLA Ops:
  0.0 20.3 %shard_map.109 = bf16[4,2,128,256]{3,2,1,0:T(8,128)(2,1)S(1)} custom-call(s32[4,2,6]{2,1,0:T(2,128)} %lists_hbm.1, s32[1,4]{1,0:T(1,128)} %strips_hbm.1, bf16[4,2,128,256]{3,2,1,0:T(8,128)(2,1)} %slip_hbm.1, bf16[4,2,6,128,128]{4,3,2,1,0:T(8,128)(2,1)} %near_hbm.1, bf16[4,2,64,128]{3,2,1,0:T(8,128)(2,1)} %source_hbm.1, bf16[4,2,64,128]{3,2,1,0:T(8,128)(2,1)} %target_hbm.1, ...), custom_call_target="tpu_custom_call" | custom-call | tf_op jit(solution)/shard_map/pallas_call | solution.py:331
  20.3 0.8 %copy.13 = bf16[4,2,128,256]{3,2,1,0:T(8,128)(2,1)} copy(bf16[4,2,128,256]{3,2,1,0:T(8,128)(2,1)S(1)} %shard_map.109) | data formatting | bytes 1048576

commit v3 on v2

--- a/solution.py
+++ b/solution.py
@@ -53,7 +53,7 @@
     strip_up,
     strip_down,
     coupling,
-    acc,
+    falls,
     part_send,
     part_recv,
     tops,
@@ -93,7 +93,7 @@
                 (slip_hbm, pad.at[pl.ds(1, along), pl.ds(1, dip)]),
                 (lists_hbm, lists),
                 (strips_hbm, strips),
-                (near_hbm, near.at[:, :, pl.ds(0, n_near)]),
+                (near_hbm, near),
                 (coupling_hbm, coupling),
                 (strip_down_hbm, strip_down),
                 (down_hbm, down),
@@ -150,7 +150,6 @@
         @pl.when(jnp.logical_not(has[side]))
         def _():
             pad[pl.ds(at, 1)] = jnp.zeros((1,) + pad.shape[1:], pad.dtype)
-    near[:, :, n_near] = jnp.zeros((along, dip) + near.shape[3:], near.dtype)
 
     leaves = [(g, h) for g in range(along) for h in range(dip)]
     loads[0].wait()
@@ -192,26 +191,6 @@
     for load in loads[4:7]:
         load.wait()
 
-    def place(g, h, q):
-        index = n_near
-        for n in range(n_near):
-            index = jnp.where(lists[g, h, n] == q, n, index)
-        return index
-
-    def wave(g, h, wanted):
-        found = [
-            (q, g + q // 3, h + q % 3)
-            for q in range(9)
-            if wanted == (1 <= g + q // 3 <= along, 1 <= h + q % 3 <= dip)
-        ]
-        if not found:
-            return None
-        blocks = jnp.concatenate([near[g, h, place(g, h, q)] for q, _, _ in found], axis=1)
-        fields = jnp.concatenate([pad[a, b] for _, a, b in found], axis=0)
-        return dot(blocks, fields)
-
-    for g, h in leaves[: len(leaves) // 2]:
-        acc[g, h] = wave(g, h, (True, True))
 
     for j in range(1, n_col):
         part(j).wait_recv()
@@ -240,37 +219,20 @@
             pl.when(jnp.logical_and(has[side], has[edge]))(lambda: corner(side, edge).start())
 
 
-    for g, h in leaves[len(leaves) // 2 :]:
-        acc[g, h] = wave(g, h, (True, True))
-
     for j in range(1, n_row):
         top(j, lax.rem(row + n_row - j, n_row)).wait_recv()
     chosen = jnp.concatenate([tops[strips[0, a]] for a in range(n_far)], axis=0)
     c_high, c_low = split(dot(pair_high[...], chosen) + dot(pair_low[...], chosen))
-    falls = dot(fall[...], jnp.concatenate([c_high, c_high, c_low], axis=0)).astype(BF16)
+    falls[...] = dot(fall[...], jnp.concatenate([c_high, c_high, c_low], axis=0)).astype(BF16).reshape(falls.shape)
 
     for g, n in later_rim:
         for side in "WE":
             pl.when(has[back[side]])(lambda: rim(side, g, n).wait_recv())
-    for g, h in leaves:
-        acc[g, h] += wave(g, h, (True, False))
     for side in "NS":
         pl.when(has[back[side]])(lambda: strike(side).wait_recv())
-    for g, h in leaves:
-        if g in (0, along - 1):
-            acc[g, h] += wave(g, h, (False, True))
-
     def result(g, h):
         return pltpu.make_async_copy(out.at[g, h], out_hbm.at[g, h], out_sems.at[g, h])
 
-    def finish(g, h, value):
-        k = g * dip + h
-        out[g, h] = (value + dot(spread[g, h], falls[k * rank : (k + 1) * rank])).astype(out.dtype)
-        result(g, h).start()
-
-    for g, h in leaves:
-        if g not in (0, along - 1):
-            finish(g, h, acc[g, h])
     for g, n in first_rim + later_rim:
         for side in "WE":
             pl.when(has[side])(lambda: rim(side, g, n).wait_send())
@@ -285,9 +247,16 @@
     for edge in "WE":
         for side in "NS":
             pl.when(jnp.logical_and(has[back[side]], has[edge]))(lambda: corner(side, edge).wait_recv())
-    for g, h in leaves:
-        if g in (0, along - 1):
-            finish(g, h, acc[g, h] + wave(g, h, (False, False)))
+
+    @pl.loop(0, along)
+    def _(g):
+        for h in range(dip):
+            places = [lists[g, h, n] for n in range(n_near)]
+            fields = jnp.concatenate([pad[g + q // 3, h + q % 3] for q in places], axis=0)
+            blocks = jnp.concatenate([near[g, h, n] for n in range(n_near)], axis=1)
+            value = dot(blocks, fields) + dot(spread[g, h], falls[g, h])
+            out[g, h] = value.astype(out.dtype)
+            result(g, h).start()
 
     for g, h in leaves:
         result(g, h).wait()
@@ -338,7 +307,7 @@
             pltpu.SMEM(strip_lists.shape, jnp.int32),
             pltpu.VMEM(slip_rate.shape, BF16),
             pltpu.VMEM((along + 2, dip + 2, leaf, members), BF16),
-            pltpu.VMEM((along, dip, n_near + 1, leaf, leaf), BF16),
+            pltpu.VMEM(near_blocks.shape, BF16),
             pltpu.VMEM(source_basis.shape, BF16),
             pltpu.VMEM(target_basis.shape, BF16),
             pltpu.VMEM(leaf_up.shape, F32),
@@ -346,7 +315,7 @@
             pltpu.VMEM(strip_up.shape, F32),
             pltpu.VMEM(strip_down.shape, F32),
             pltpu.VMEM(coupling.shape, F32),
-            pltpu.VMEM(slip_rate.shape, F32),
+            pltpu.VMEM((along, dip, rank, members), BF16),
             pltpu.VMEM((rank, members), BF16),
             pltpu.VMEM((n_col, rank, members), BF16),
             pltpu.VMEM((n_row, rank, members), BF16),

time: 21.2 us -> 21.6 us (1.019)
  Pallas kernels: 20.3 us -> 20.6 us
    pallas_call x1, Pallas kernels: 20.3 us -> 20.6 us  [body(): pl.pallas_call(functools.partial(kernel, n_row, n_col), out_shape=jax.Sha...]
where the time goes in v3:
time: 21.6 us; the launch traced here: 21.4 us
  Pallas kernels  20.6 us (95%)
  local copies, waits for them, and re-layouts  0.8 us (4%)
    pallas_call x1, Pallas kernels, body(): pl.pallas_call(functools.partial(kernel, n_row, n_col), out_shape=jax.Sha...  20.6 us
    unnamed x1, local copies, waits for them, and re-layouts  0.8 us

profile of v3, /device:TPU:0, one launch (start us, length us, event | category | flops | bytes accessed | tf_op | source)
XLA Modules:
  0.0 21.4 jit_solution(11300054354121244511)
XLA Ops:
  0.0 20.6 %shard_map.109 = bf16[4,2,128,256]{3,2,1,0:T(8,128)(2,1)S(1)} custom-call(s32[4,2,6]{2,1,0:T(2,128)} %lists_hbm.1, s32[1,4]{1,0:T(1,128)} %strips_hbm.1, bf16[4,2,128,256]{3,2,1,0:T(8,128)(2,1)} %slip_hbm.1, bf16[4,2,6,128,128]{4,3,2,1,0:T(8,128)(2,1)} %near_hbm.1, bf16[4,2,64,128]{3,2,1,0:T(8,128)(2,1)} %source_hbm.1, bf16[4,2,64,128]{3,2,1,0:T(8,128)(2,1)} %target_hbm.1, ...), custom_call_target="tpu_custom_call" | custom-call | tf_op jit(solution)/shard_map/pallas_call | solution.py:300
  20.6 0.8 %copy.13 = bf16[4,2,128,256]{3,2,1,0:T(8,128)(2,1)} copy(bf16[4,2,128,256]{3,2,1,0:T(8,128)(2,1)S(1)} %shard_map.109) | data formatting | bytes 1048576

commit v4 on v2

--- a/solution.py
+++ b/solution.py
@@ -140,6 +140,8 @@
     for g, n in first_rim:
         for side in "WE":
             pl.when(has[side])(lambda: rim(side, g, n).start())
+    for side in "NS":
+        pl.when(has[side])(lambda: strike(side).start())
 
     empty = jnp.zeros((along + 2, 1) + pad.shape[2:], pad.dtype)
     for side, at in (("W", 0), ("E", dip + 1)):
@@ -175,8 +177,9 @@
 
     for j in range(1, n_col):
         part(j).start()
-    for side in "NS":
-        pl.when(has[side])(lambda: strike(side).start())
+    for g, n in later_rim:
+        for side in "WE":
+            pl.when(has[side])(lambda: rim(side, g, n).start())
 
     for load in loads[7:]:
         load.wait()
@@ -229,9 +232,6 @@
 
     for j in range(1, n_row):
         top(j, row).start()
-    for g, n in later_rim:
-        for side in "WE":
-            pl.when(has[side])(lambda: rim(side, g, n).start())
     for g, n in first_rim:
         for side in "WE":
             pl.when(has[back[side]])(lambda: rim(side, g, n).wait_recv())

time: 21.2 us -> 21.2 us (level)
  no operation moved by 1% of the time
where the time goes in v4:
time: 21.2 us; the launch traced here: 21.1 us
  Pallas kernels  20.3 us (96%)
  local copies, waits for them, and re-layouts  0.8 us (4%)
    pallas_call x1, Pallas kernels, body(): pl.pallas_call(functools.partial(kernel, n_row, n_col), out_shape=jax.Sha...  20.3 us
    unnamed x1, local copies, waits for them, and re-layouts  0.8 us

profile of v4, /device:TPU:0, one launch (start us, length us, event | category | flops | bytes accessed | tf_op | source)
XLA Modules:
  0.0 21.1 jit_solution(5031940557464995564)
XLA Ops:
  0.0 20.3 %shard_map.109 = bf16[4,2,128,256]{3,2,1,0:T(8,128)(2,1)S(1)} custom-call(s32[4,2,6]{2,1,0:T(2,128)} %lists_hbm.1, s32[1,4]{1,0:T(1,128)} %strips_hbm.1, bf16[4,2,128,256]{3,2,1,0:T(8,128)(2,1)} %slip_hbm.1, bf16[4,2,6,128,128]{4,3,2,1,0:T(8,128)(2,1)} %near_hbm.1, bf16[4,2,64,128]{3,2,1,0:T(8,128)(2,1)} %source_hbm.1, bf16[4,2,64,128]{3,2,1,0:T(8,128)(2,1)} %target_hbm.1, ...), custom_call_target="tpu_custom_call" | custom-call | tf_op jit(solution)/shard_map/pallas_call | solution.py:331
  20.3 0.8 %copy.13 = bf16[4,2,128,256]{3,2,1,0:T(8,128)(2,1)} copy(bf16[4,2,128,256]{3,2,1,0:T(8,128)(2,1)S(1)} %shard_map.109) | data formatting | bytes 1048576

commit v5 on v4

--- a/solution.py
+++ b/solution.py
@@ -243,23 +243,23 @@
     for g, h in leaves[len(leaves) // 2 :]:
         acc[g, h] = wave(g, h, (True, True))
 
+    for g, n in later_rim:
+        for side in "WE":
+            pl.when(has[back[side]])(lambda: rim(side, g, n).wait_recv())
+    for g, h in leaves:
+        acc[g, h] += wave(g, h, (True, False))
+    for side in "NS":
+        pl.when(has[back[side]])(lambda: strike(side).wait_recv())
+    for g, h in leaves:
+        if g in (0, along - 1):
+            acc[g, h] += wave(g, h, (False, True))
+
     for j in range(1, n_row):
         top(j, lax.rem(row + n_row - j, n_row)).wait_recv()
     chosen = jnp.concatenate([tops[strips[0, a]] for a in range(n_far)], axis=0)
     c_high, c_low = split(dot(pair_high[...], chosen) + dot(pair_low[...], chosen))
     falls = dot(fall[...], jnp.concatenate([c_high, c_high, c_low], axis=0)).astype(BF16)
 
-    for g, n in later_rim:
-        for side in "WE":
-            pl.when(has[back[side]])(lambda: rim(side, g, n).wait_recv())
-    for g, h in leaves:
-        acc[g, h] += wave(g, h, (True, False))
-    for side in "NS":
-        pl.when(has[back[side]])(lambda: strike(side).wait_recv())
-    for g, h in leaves:
-        if g in (0, along - 1):
-            acc[g, h] += wave(g, h, (False, True))
-
     def result(g, h):
         return pltpu.make_async_copy(out.at[g, h], out_hbm.at[g, h], out_sems.at[g, h])
 
@@ -271,6 +271,13 @@
     for g, h in leaves:
         if g not in (0, along - 1):
             finish(g, h, acc[g, h])
+    for edge in "WE":
+        for side in "NS":
+            pl.when(jnp.logical_and(has[back[side]], has[edge]))(lambda: corner(side, edge).wait_recv())
+    for g, h in leaves:
+        if g in (0, along - 1):
+            finish(g, h, acc[g, h] + wave(g, h, (False, False)))
+
     for g, n in first_rim + later_rim:
         for side in "WE":
             pl.when(has[side])(lambda: rim(side, g, n).wait_send())
@@ -282,13 +289,6 @@
         part(j).wait_send()
     for j in range(1, n_row):
         top(j, row).wait_send()
-    for edge in "WE":
-        for side in "NS":
-            pl.when(jnp.logical_and(has[back[side]], has[edge]))(lambda: corner(side, edge).wait_recv())
-    for g, h in leaves:
-        if g in (0, along - 1):
-            finish(g, h, acc[g, h] + wave(g, h, (False, False)))
-
     for g, h in leaves:
         result(g, h).wait()
 

time: 21.2 us -> 20.8 us (0.981)
  Pallas kernels: 20.3 us -> 19.8 us
    pallas_call x1, Pallas kernels: 20.3 us -> 19.8 us  [body(): pl.pallas_call(functools.partial(kernel, n_row, n_col), out_shape=jax.Sha...]
where the time goes in v5:
time: 20.8 us; the launch traced here: 20.7 us
  Pallas kernels  19.8 us (95%)
  local copies, waits for them, and re-layouts  0.8 us (4%)
    pallas_call x1, Pallas kernels, body(): pl.pallas_call(functools.partial(kernel, n_row, n_col), out_shape=jax.Sha...  19.8 us
    unnamed x1, local copies, waits for them, and re-layouts  0.8 us

profile of v5, /device:TPU:0, one launch (start us, length us, event | category | flops | bytes accessed | tf_op | source)
XLA Modules:
  0.0 20.7 jit_solution(13871054301514946044)
XLA Ops:
  0.0 19.8 %shard_map.109 = bf16[4,2,128,256]{3,2,1,0:T(8,128)(2,1)S(1)} custom-call(s32[4,2,6]{2,1,0:T(2,128)} %lists_hbm.1, s32[1,4]{1,0:T(1,128)} %strips_hbm.1, bf16[4,2,128,256]{3,2,1,0:T(8,128)(2,1)} %slip_hbm.1, bf16[4,2,6,128,128]{4,3,2,1,0:T(8,128)(2,1)} %near_hbm.1, bf16[4,2,64,128]{3,2,1,0:T(8,128)(2,1)} %source_hbm.1, bf16[4,2,64,128]{3,2,1,0:T(8,128)(2,1)} %target_hbm.1, ...), custom_call_target="tpu_custom_call" | custom-call | tf_op jit(solution)/shard_map/pallas_call | solution.py:331
  19.9 0.8 %copy.13 = bf16[4,2,128,256]{3,2,1,0:T(8,128)(2,1)} copy(bf16[4,2,128,256]{3,2,1,0:T(8,128)(2,1)S(1)} %shard_map.109) | data formatting | bytes 1048576

commit v6 on v5

--- a/solution.py
+++ b/solution.py
@@ -135,14 +135,6 @@
     first_rim = [(0, 1), (along - 1, 1)]
     later_rim = [(1, along - 2)]
 
-    pl.semaphore_wait(barrier, n_row + n_col - 2)
-
-    for g, n in first_rim:
-        for side in "WE":
-            pl.when(has[side])(lambda: rim(side, g, n).start())
-    for side in "NS":
-        pl.when(has[side])(lambda: strike(side).start())
-
     empty = jnp.zeros((along + 2, 1) + pad.shape[2:], pad.dtype)
     for side, at in (("W", 0), ("E", dip + 1)):
         @pl.when(jnp.logical_not(has[side]))
@@ -175,8 +167,15 @@
             device_id={"col": to}, device_id_type=MESH,
         )
 
+    pl.semaphore_wait(barrier, n_row + n_col - 2)
+
     for j in range(1, n_col):
         part(j).start()
+    for g, n in first_rim:
+        for side in "WE":
+            pl.when(has[side])(lambda: rim(side, g, n).start())
+    for side in "NS":
+        pl.when(has[side])(lambda: strike(side).start())
     for g, n in later_rim:
         for side in "WE":
             pl.when(has[side])(lambda: rim(side, g, n).start())

time: 20.8 us -> 18.9 us (0.909)
  Pallas kernels: 19.8 us -> 17.9 us
    pallas_call x1, Pallas kernels: 19.8 us -> 17.9 us  [body(): pl.pallas_call(functools.partial(kernel, n_row, n_col), out_shape=jax.Sha...]
where the time goes in v6:
time: 18.9 us; the launch traced here: 18.7 us
  Pallas kernels  17.9 us (95%)
  local copies, waits for them, and re-layouts  0.8 us (4%)
    pallas_call x1, Pallas kernels, body(): pl.pallas_call(functools.partial(kernel, n_row, n_col), out_shape=jax.Sha...  17.9 us
    unnamed x1, local copies, waits for them, and re-layouts  0.8 us

profile of v6, /device:TPU:0, one launch (start us, length us, event | category | flops | bytes accessed | tf_op | source)
XLA Modules:
  0.0 18.7 jit_solution(2975084049756392404)
XLA Ops:
  0.0 17.9 %shard_map.109 = bf16[4,2,128,256]{3,2,1,0:T(8,128)(2,1)S(1)} custom-call(s32[4,2,6]{2,1,0:T(2,128)} %lists_hbm.1, s32[1,4]{1,0:T(1,128)} %strips_hbm.1, bf16[4,2,128,256]{3,2,1,0:T(8,128)(2,1)} %slip_hbm.1, bf16[4,2,6,128,128]{4,3,2,1,0:T(8,128)(2,1)} %near_hbm.1, bf16[4,2,64,128]{3,2,1,0:T(8,128)(2,1)} %source_hbm.1, bf16[4,2,64,128]{3,2,1,0:T(8,128)(2,1)} %target_hbm.1, ...), custom_call_target="tpu_custom_call" | custom-call | tf_op jit(solution)/shard_map/pallas_call | solution.py:330
  17.9 0.8 %copy.13 = bf16[4,2,128,256]{3,2,1,0:T(8,128)(2,1)} copy(bf16[4,2,128,256]{3,2,1,0:T(8,128)(2,1)S(1)} %shard_map.109) | data formatting | bytes 1048576
